TPU v7x, 512 devices: a whole 4x8x8 slice. The times are simulated.
512 devices in a mesh: gx: 32 (over z_lo, y, core), gy: 16 (over z_hi, x).
Axes of the slice: x: 4, y: 8, z: 8 (z_hi: 4, z_lo: 2; z = z_hi * 2 + z_lo), core: 2. Of those that a mesh axis runs over, the one named last changes fastest.
Arguments:
- node_feats: bfloat16 [32, 16, 128, 64], P('gx', 'gy'), may hold values from -6 to 6
- positions: float32 [32, 16, 3, 64], P('gx', 'gy'), may hold values from 0 to 50, as said below
- species: int32 [32, 16, 64], P('gx', 'gy'), may hold values from 0 to 9
- occupied: int32 [32, 16, 64], P('gx', 'gy'), may hold values 0 or 1
- energy_shift: float32 [10], replicated, may hold values from -4 to 4
- energy_scale: float32 [10], replicated, may hold values from 0.1 to 1.9
- radial_weight: float32 [4, 3, 128], replicated, may hold values from -1.8 to 1.8
- mix_weight: bfloat16 [384, 128], replicated, may hold values from -0.3125 to 0.3125
- readout: float32 [128], replicated, may hold values from -0.5 to 0.5
Outputs:
- atom_energy: float32 [32, 16, 64], P('gx', 'gy')
- forces: float32 [32, 16, 3, 64], P('gx', 'gy')
- feature_grad: float32 [32, 16, 128, 64], P('gx', 'gy')
Inputs may be any that keep to these rules, and one draw needn't show every extreme that they name: `positions`: each coordinate is measured from its own cell's corner, the first two along the grid's dimensions (up to 5), the third across the slab (up to 50); no two slots lie closer than 0.9.
All inputs are finite; a program needn't handle non-finite values. No bound on the sum of `occupied` on one device may be relied on, other than what follows from the above.
Results may differ from a plain program's by a relative error of at most 0.0046.
Values may be sent and summed in bfloat16 or wider, within the bound.
A program may use at most 64 MiB of HBM per device.

v0:
```python
from functools import partial
import math

import jax
import jax.numpy as jnp
from jax import lax
from jax.sharding import PartitionSpec as P

NB = 4


CELL_SIDE = 5.0
CUTOFF = 5.0
OFFSET_LIST = tuple(((step_x, step_y) for step_x in (-1, 0, 1) for step_y in (-1, 0, 1)))


def extended(cells, sides, width):
    for axis, dim in sides:
        count = lax.axis_size(axis)
        head = lax.slice_in_dim(cells, 0, width, axis=dim)
        tail = lax.slice_in_dim(cells, cells.shape[dim] - width, cells.shape[dim], axis=dim)
        cells = jnp.concatenate(
            [
                lax.ppermute(tail, axis, [(i, (i + 1) % count) for i in range(count)]),
                cells,
                lax.ppermute(head, axis, [((i + 1) % count, i) for i in range(count)]),
            ],
            axis=dim,
        )
    return cells


def shifted(x, axis, by):
    size = lax.axis_size(axis)
    return lax.ppermute(x, axis, [(i, (i + by) % size) for i in range(size)])


def pair_basis(centre_pos, other_pos, shift_x, shift_y, same_cell):
    float_kind = centre_pos.dtype
    slot_count = centre_pos.shape[1]
    offset = jnp.array([shift_x * CELL_SIDE, shift_y * CELL_SIDE, 0.0], float_kind)
    relative = other_pos[:, None, :] - centre_pos[:, :, None] + offset[:, None, None]
    dist_sq = jnp.sum(relative * relative, axis=0)
    if same_cell:
        self_pair = jnp.eye(slot_count, dtype=float_kind)
        dist_sq = dist_sq + self_pair
        keep_pair = 1.0 - self_pair
    else:
        keep_pair = jnp.ones_like(dist_sq)
    distance = jnp.sqrt(dist_sq)
    unit_vec = relative / distance
    scaled = distance / CUTOFF
    poly = 1.0 - 28.0 * scaled**6 + 48.0 * scaled**7 - 21.0 * scaled**8
    envelope = jnp.where(scaled < 1.0, poly, 0.0) * keep_pair
    orders = jnp.arange(1, NB + 1).astype(float_kind)[:, None, None]
    radial = math.sqrt(2.0 / CUTOFF) * jnp.sin(orders * math.pi * scaled) / distance * envelope
    unit_x, unit_y, unit_z = (unit_vec[0], unit_vec[1], unit_vec[2])
    root_three = math.sqrt(3.0)
    root_fifteen = math.sqrt(15.0)
    harmonic = jnp.stack(
        [
            jnp.ones_like(unit_x),
            root_three * unit_x,
            root_three * unit_y,
            root_three * unit_z,
            root_fifteen * unit_x * unit_y,
            root_fifteen * unit_y * unit_z,
            0.5 * math.sqrt(5.0) * (3.0 * unit_z * unit_z - 1.0),
            root_fifteen * unit_x * unit_z,
            0.5 * root_fifteen * (unit_x * unit_x - unit_y * unit_y),
        ]
    )
    return (radial[:, None] * harmonic[None]).reshape(-1, slot_count, slot_count)


def expand_radial(radial_weight):
    return jnp.concatenate(
        [
            radial_weight[:, 0:1],
            jnp.repeat(radial_weight[:, 1:2], 3, axis=1),
            jnp.repeat(radial_weight[:, 2:3], 5, axis=1),
        ],
        axis=1,
    )


def messages(centre_pos, near_pos, near_feat, picks):
    total = None
    for number, shift_x, shift_y in picks:
        basis = pair_basis(
            centre_pos, near_pos[number], shift_x, shift_y, shift_x == 0 and shift_y == 0
        )
        term = jnp.einsum(
            "kij,cj->kic",
            basis.astype(jnp.bfloat16),
            near_feat[number],
            preferred_element_type=jnp.float32,
        )
        total = term if total is None else total + term
    return total


def cell_tail(
    total,
    centre_pos,
    species_row,
    mask_row,
    near_pos,
    near_feat,
    energy_shift,
    energy_scale,
    radial_weight,
    mix_weight,
    readout,
):
    channels = readout.shape[0]
    slot_count = centre_pos.shape[1]
    wide = expand_radial(radial_weight)
    split = total.reshape(wide.shape[0], 9, slot_count, channels)
    amp = jnp.sum(wide[:, :, None, :] * split, axis=0)
    invariants = jnp.concatenate(
        [amp[0], jnp.sum(amp[1:4] * amp[1:4], axis=0), jnp.sum(amp[4:9] * amp[4:9], axis=0)], axis=1
    ).astype(jnp.bfloat16)
    pre = jnp.dot(invariants, mix_weight, preferred_element_type=jnp.float32)
    sigma = jax.nn.sigmoid(pre)
    onehot = (
        species_row[:, None] == jnp.arange(energy_shift.shape[0], dtype=jnp.int32)[None, :]
    ).astype(jnp.float32)
    shift_row = jnp.sum(onehot * energy_shift[None, :], axis=1)
    scale_row = jnp.sum(onehot * energy_scale[None, :], axis=1)
    mask_float = mask_row.astype(jnp.float32)
    energy = mask_float * (shift_row + scale_row * jnp.sum(pre * sigma * readout[None, :], axis=1))
    coef = mask_float * scale_row
    dpre = (coef[:, None] * readout[None, :] * sigma * (1.0 + pre * (1.0 - sigma))).astype(
        jnp.bfloat16
    )
    dinv = jnp.dot(dpre, mix_weight.T, preferred_element_type=jnp.float32)
    damp = jnp.concatenate(
        [
            dinv[None, :, :channels],
            2.0 * amp[1:4] * dinv[None, :, channels : 2 * channels],
            2.0 * amp[4:9] * dinv[None, :, 2 * channels :],
        ],
        axis=0,
    )
    coeff = (
        (wide[:, :, None, :] * damp[None]).reshape(-1, slot_count, channels).astype(jnp.bfloat16)
    )
    grad_centre = jnp.zeros((3, slot_count), jnp.float32)
    pieces = []
    for number, (shift_x, shift_y) in enumerate(OFFSET_LIST):
        local_basis = partial(
            pair_basis, shift_x=shift_x, shift_y=shift_y, same_cell=shift_x == 0 and shift_y == 0
        )
        basis, pull_back = jax.vjp(local_basis, centre_pos, near_pos[number])
        dbasis = jnp.einsum(
            "kic,cj->kij", coeff, near_feat[number], preferred_element_type=jnp.float32
        )
        grad_i, grad_j = pull_back(dbasis)
        dfeat = jnp.einsum(
            "kij,kic->cj", basis.astype(jnp.bfloat16), coeff, preferred_element_type=jnp.float32
        )
        grad_centre = grad_centre + grad_i
        pieces.append(jnp.concatenate([dfeat, grad_j], axis=0))
    return (energy, grad_centre, jnp.stack(pieces))


def neighbours(padded, cells_x, cells_y):
    stacked = jnp.stack(
        [
            padded[1 + step_x : 1 + step_x + cells_x, 1 + step_y : 1 + step_y + cells_y]
            for step_x, step_y in OFFSET_LIST
        ],
        axis=2,
    )
    return stacked.reshape((cells_x * cells_y, len(OFFSET_LIST)) + padded.shape[2:])


def fetch_ghosts(masked, positions):
    feat_pad = extended(masked, (("gx", 0), ("gy", 1)), 1)
    pos_pad = extended(positions, (("gx", 0), ("gy", 1)), 1)
    return (feat_pad, pos_pad)


def fold_back(gathered):
    for shift_by in (1, -1):
        strip = gathered[:, -1:] if shift_by == 1 else gathered[:, :1]
        arrived = shifted(strip, "gy", shift_by)
        if shift_by == 1:
            gathered = gathered.at[:, 1:2].add(arrived)
        else:
            gathered = gathered.at[:, -2:-1].add(arrived)
    for shift_by in (1, -1):
        strip = gathered[-1:, 1:-1] if shift_by == 1 else gathered[:1, 1:-1]
        arrived = shifted(strip.astype(jnp.bfloat16), "gx", shift_by).astype(strip.dtype)
        if shift_by == 1:
            gathered = gathered.at[1:2, 1:-1].add(arrived)
        else:
            gathered = gathered.at[-2:-1, 1:-1].add(arrived)
    return gathered[1:-1, 1:-1]


def shards(
    node_feats,
    positions,
    species,
    occupied,
    energy_shift,
    energy_scale,
    radial_weight,
    mix_weight,
    readout,
):
    cells_x, cells_y, channels, slot_count = node_feats.shape
    cell_total = cells_x * cells_y
    mask_float = occupied.astype(jnp.float32)
    masked = node_feats * occupied[:, :, None, :].astype(jnp.bfloat16)
    pos_cells = positions.reshape(cell_total, 3, slot_count)
    all_picks = tuple(
        ((number, shift_x, shift_y) for number, (shift_x, shift_y) in enumerate(OFFSET_LIST))
    )
    feat_pad, pos_pad = fetch_ghosts(masked, positions)
    near_feat = neighbours(feat_pad, cells_x, cells_y)
    near_pos = neighbours(pos_pad, cells_x, cells_y)

    def every_part(inputs):
        return messages(inputs[0], inputs[1], inputs[2], all_picks)

    total = lax.map(every_part, (pos_cells, near_pos, near_feat))

    def per_cell(inputs):
        cell_sum, centre_pos, species_row, mask_row, cell_pos, cell_feat = inputs
        return cell_tail(
            cell_sum,
            centre_pos,
            species_row,
            mask_row,
            cell_pos,
            cell_feat,
            energy_shift,
            energy_scale,
            radial_weight,
            mix_weight,
            readout,
        )

    energy, grad_centre, pieces = lax.map(
        per_cell,
        (
            total,
            pos_cells,
            species.reshape(cell_total, slot_count),
            occupied.reshape(cell_total, slot_count),
            near_pos,
            near_feat,
        ),
    )
    pieces = pieces.reshape(cells_x, cells_y, len(OFFSET_LIST), channels + 3, slot_count)
    gathered = jnp.zeros((cells_x + 2, cells_y + 2, channels + 3, slot_count), jnp.float32)
    for number, (shift_x, shift_y) in enumerate(OFFSET_LIST):
        gathered = gathered.at[
            1 + shift_x : 1 + shift_x + cells_x, 1 + shift_y : 1 + shift_y + cells_y
        ].add(pieces[:, :, number])
    owned = fold_back(gathered)
    forces = -(grad_centre.reshape(cells_x, cells_y, 3, slot_count) + owned[:, :, channels:])
    feature_grad = owned[:, :, :channels] * mask_float[:, :, None, :]
    return (energy.reshape(cells_x, cells_y, slot_count), forces, feature_grad)


def solution(mesh):
    placed = (
        P("gx", "gy", None, None),
        P("gx", "gy", None, None),
        P("gx", "gy", None),
        P("gx", "gy", None),
        P(),
        P(),
        P(),
        P(),
        P(),
    )
    return jax.shard_map(
        shards,
        mesh=mesh,
        in_specs=placed,
        out_specs=(P("gx", "gy", None), P("gx", "gy", None, None), P("gx", "gy", None, None)),
        check_vma=False,
    )
```

profile of v0, /device:TPU:25, one launch (start us, length us, event | category | flops | bytes accessed | tf_op | source)
XLA Modules:
  0.0 117.1 jit_solution(10011016660612545842)
XLA Ops:
  0.7 5.1 %collective-permute-start = (f32[1,1,3,64]{3,1,2,0:T(1,128)}, f32[1,1,3,64]{3,1,2,0:T(1,128)S(1)}, u32[]{:S(2)}, u32[]{:S(2)}) collective-permute-start(f32[1,1,3,64]{3,1,2,0:T(1,128)} %param.54), channel_id=1, source_target_pairs={{0,16},{16,32},{32,48},{48,64},{64,80},{80,96},{96,112},{112,128},... | collective-permute-start | bytes 2312 | tf_op jit(solution)/shard_map/ppermute | solution.py:24
  5.8 1.9 %collective-permute-start.1 = (f32[1,1,3,64]{3,1,2,0:T(1,128)}, f32[1,1,3,64]{3,1,2,0:T(1,128)S(1)}, u32[]{:S(2)}, u32[]{:S(2)}) collective-permute-start(f32[1,1,3,64]{3,1,2,0:T(1,128)} %param.54), channel_id=1, source_target_pairs={{16,0},{32,16},{48,32},{64,48},{80,64},{96,80},{112,96},{128,112},... | collective-permute-start | bytes 2312 | tf_op jit(solution)/shard_map/ppermute | solution.py:26
  7.7 0.7 convert_bitcast_fusion.1
  8.5 0.8 broadcast_multiply_fusion.9
  9.2 4.8 %collective-permute-start.3 = (bf16[1,1,128,64]{2,3,1,0:T(8,128)(2,1)S(1)}, bf16[1,1,128,64]{2,3,1,0:T(8,128)(2,1)S(1)}, u32[]{:S(2)}, u32[]{:S(2)}) collective-permute-start(bf16[1,1,128,64]{2,3,1,0:T(8,128)(2,1)S(1)} %broadcast_multiply_fusion.9), channel_id=1, source_target_pairs={{0,16},{16,32},{32,48},{48,64},{64,80},{80,96},{96,112},{112,128},... | collective-permute-start | bytes 49160 | tf_op jit(solution)/shard_map/ppermute | solution.py:24
  14.1 1.9 %collective-permute-start.4 = (bf16[1,1,128,64]{2,3,1,0:T(8,128)(2,1)S(1)}, bf16[1,1,128,64]{2,3,1,0:T(8,128)(2,1)S(1)}, u32[]{:S(2)}, u32[]{:S(2)}) collective-permute-start(bf16[1,1,128,64]{2,3,1,0:T(8,128)(2,1)S(1)} %broadcast_multiply_fusion.9), channel_id=1, source_target_pairs={{16,0},{32,16},{48,32},{64,48},{80,64},{96,80},{112,96},{128,112},... | collective-permute-start | bytes 49160 | tf_op jit(solution)/shard_map/ppermute | solution.py:26
  16.1 0.7 fusion.409
  16.9 0.8 select_reduce_fusion
  17.6 0.7 fusion.393
  18.3 0.6 fusion.412
  18.9 1.4 %and_reduce_fusion = pred[]{:T(512)} fusion(s32[4]{0:T(128)} %constant.551.clone.1, s32[1]{0:T(128)} %constant.550.clone.1, s32[2]{0:T(128)S(1)} %iota_multiply_fusion), kind=kLoop, calls=%fused_computation.809 | loop fusion | flops 23 | bytes 29 | tf_op jit(solution)/shard_map/reduce.15
  20.3 0.6 fusion.413
  20.9 0.7 constant_dynamic-update-slice_fusion.1
  21.6 12.8 %collective-permute-start.6 = (f32[3,1,3,64]{3,1,2,0:T(1,128)S(1)}, f32[3,1,3,64]{3,1,2,0:T(1,128)S(1)}, u32[]{:S(2)}, u32[]{:S(2)}) collective-permute-start(f32[3,1,3,64]{3,1,2,0:T(1,128)S(1)} %constant_dynamic-update-slice_fusion), channel_id=1, source_target_pairs={{1,0},{2,1},{3,2},{4,3},{5,4},{6,5},{7,6},{8,7},{9,8},{10,9},{11,1... | collective-permute-start | bytes 6920 | tf_op jit(solution)/shard_map/ppermute | solution.py:26
  34.4 0.7 copy.187
  35.1 1.9 %collective-permute-start.2 = (f32[3,1,3,64]{3,1,2,0:T(1,128)S(1)}, f32[3,1,3,64]{3,1,2,0:T(1,128)S(1)}, u32[]{:S(2)}, u32[]{:S(2)}) collective-permute-start(f32[3,1,3,64]{3,1,2,0:T(1,128)S(1)} %constant_dynamic-update-slice_fusion), channel_id=1, source_target_pairs={{0,1},{1,2},{2,3},{3,4},{4,5},{5,6},{6,7},{7,8},{8,9},{9,10},{10,1... | collective-permute-start | bytes 6920 | tf_op jit(solution)/shard_map/ppermute | solution.py:24
  37.1 6.6 %collective-permute-done.2 = f32[3,1,3,64]{3,1,2,0:T(1,128)S(1)} collective-permute-done((f32[3,1,3,64]{3,1,2,0:T(1,128)S(1)}, f32[3,1,3,64]{3,1,2,0:T(1,128)S(1)}, u32[]{:S(2)}, u32[]{:S(2)}) %collective-permute-start.2) | collective-permute-done | bytes 2336 | tf_op jit(solution)/shard_map/ppermute | solution.py:24
  43.7 1.0 multiply_reduce_fusion.41
  46.2 2.7 %fusion.111 = (f32[4,64,64]{2,1,0:T(8,128)S(1)}, f32[4,64,64]{2,1,0:T(8,128)S(1)}, f32[4,64,64]{2,1,0:T(8,128)S(1)}, f32[4,64,64]{2,1,0:T(8,128)S(1)}, f32[4,64,64]{2,1,0:T(8,128)S(1)}, /*index=5*/f32[4,64,64]{2,1,0:T(8,128)S(1)}) fusion(f32[64,64]{1,0:T(8,128)S(1)} %get-tuple-element.434, f32[64,64]{1,0:T(8,128)S(1)} %get-tuple-element.435, ...), kind=kLoop, calls=%fused_computation.325 | loop fusion | flops 393216 | bytes 688144 | tf_op jit(solution)/shard_map/while/body/eval_jaxpr/mul | solution.py:56
  49.8 1.4 %fusion.116 = (f32[4,64,64]{2,1,0:T(8,128)S(1)}, f32[4,64,64]{2,1,0:T(8,128)S(1)}, f32[4,64,64]{2,1,0:T(8,128)S(1)}) fusion(f32[64,64]{1,0:T(8,128)S(1)} %get-tuple-element.442, f32[64,64]{1,0:T(8,128)S(1)} %get-tuple-element.443, f32[64,64]{1,0:T(8,128)S(1)} %get-tuple-element.441, f32[4]{0:T(128)S(1)} %convert_multiply_fusion, ...), kind=kLoop, calls=%fused_computation.330 | loop fusion | flops 196608 | bytes 344080 | tf_op jit(solution)/shard_map/while/body/eval_jaxpr/mul | solution.py:56
  52.4 1.9 %collective-permute-start.7 = (bf16[3,1,128,64]{2,3,1,0:T(8,128)(2,1)S(1)}, bf16[3,1,128,64]{2,3,1,0:T(8,128)(2,1)S(1)}, u32[]{:S(2)}, u32[]{:S(2)}) collective-permute-start(bf16[3,1,128,64]{2,3,1,0:T(8,128)(2,1)S(1)} %pad_maximum_fusion.1), channel_id=1, source_target_pairs={{1,0},{2,1},{3,2},{4,3},{5,4},{6,5},{7,6},{8,7},{9,8},{10,9},{11,1... | collective-permute-start | bytes 147464 | tf_op jit(solution)/shard_map/ppermute | solution.py:26
  54.3 3.5 %collective-permute-start.5 = (bf16[3,1,128,64]{2,3,1,0:T(8,128)(2,1)S(1)}, bf16[3,1,128,64]{2,3,1,0:T(8,128)(2,1)S(1)}, u32[]{:S(2)}, u32[]{:S(2)}) collective-permute-start(bf16[3,1,128,64]{2,3,1,0:T(8,128)(2,1)S(1)} %pad_maximum_fusion.1), channel_id=1, source_target_pairs={{0,1},{1,2},{2,3},{3,4},{4,5},{5,6},{6,7},{7,8},{8,9},{9,10},{10,1... | collective-permute-start | bytes 147464 | tf_op jit(solution)/shard_map/ppermute | solution.py:24
  58.4 5.7 %collective-permute-done.5 = bf16[3,1,128,64]{2,3,1,0:T(8,128)(2,1)S(1)} collective-permute-done((bf16[3,1,128,64]{2,3,1,0:T(8,128)(2,1)S(1)}, bf16[3,1,128,64]{2,3,1,0:T(8,128)(2,1)S(1)}, u32[]{:S(2)}, u32[]{:S(2)}) %collective-permute-start.5) | collective-permute-done | bytes 49184 | tf_op jit(solution)/shard_map/ppermute | solution.py:24
  66.2 0.4 copy-done.10
  68.1 0.4 multiply_reduce_fusion.8
  71.1 0.4 multiply_reduce_fusion.4
  71.6 0.4 multiply_reduce_fusion
  72.1 0.4 multiply_reduce_fusion.2
  72.5 2.1 %fusion.94 = (f32[64,64]{1,0:T(8,128)S(1)}, f32[64,64]{1,0:T(8,128)S(1)}, f32[64,64]{1,0:T(8,128)S(1)}, f32[64,64]{1,0:T(8,128)S(1)}, f32[64,64]{1,0:T(8,128)S(1...) fusion(f32[4,64,64]{2,1,0:T(8,128)S(1)} %get-tuple-element.288, ...), kind=kLoop, calls=%fused_computation.264 | loop fusion | flops 651264 | bytes 540688 | tf_op jit(solution)/shard_map/while/body/eval_jaxpr/transpose(jvp())/reduce_sum | solution.py:56
  75.1 0.4 multiply_reduce_fusion.10
  75.6 0.4 multiply_reduce_fusion.6
  76.1 0.4 multiply_reduce_fusion.12
  76.5 1.8 %fusion.73 = (f32[64,64]{1,0:T(8,128)S(1)}, f32[64,64]{1,0:T(8,128)S(1)}, f32[64,64]{1,0:T(8,128)S(1)}, f32[64,64]{1,0:T(8,128)S(1)}, f32[64,64]{1,0:T(8,128)S(1...) fusion(f32[4,64,64]{2,1,0:T(8,128)S(1)} %get-tuple-element.294, ...), kind=kLoop, calls=%fused_computation.243 | loop fusion | flops 651264 | bytes 540688 | tf_op jit(solution)/shard_map/while/body/eval_jaxpr/transpose(jvp())/reduce_sum | solution.py:56
  78.9 0.4 multiply_reduce_fusion.16
  79.4 0.4 multiply_reduce_fusion.14
  80.4 1.8 %fusion.52 = (f32[64,64]{1,0:T(8,128)S(1)}, f32[64,64]{1,0:T(8,128)S(1)}, f32[64,64]{1,0:T(8,128)S(1)}, f32[64,64]{1,0:T(8,128)S(1)}, f32[64,64]{1,0:T(8,128)S(1...) fusion(f32[4,64,64]{2,1,0:T(8,128)S(1)} %get-tuple-element.300, ...), kind=kLoop, calls=%fused_computation.222 | loop fusion | flops 651264 | bytes 540688 | tf_op jit(solution)/shard_map/while/body/eval_jaxpr/transpose(jvp())/reduce_sum | solution.py:56
  83.5 1.3 %fusion.119 = f32[3,3,131,64]{3,2,1,0:T(8,128)S(1)} fusion(f32[3,3,131,64]{3,2,1,0:T(8,128)S(1)} %scatter-add.30, s32[]{:T(128)} %bitcast.95, s32[]{:T(128)} %bitcast.96, f32[1,1,131,64]{3,2,1,0:T(8,128)S(1)} %slice_bitcast_fusion.8, f32[1,1,9,131,64]{4,3,2,1,0:T(8,128)S(1)} %bitcast.389), kind=kLoop, calls=%fused_computation.334 | loop fusion | flops 8384 | bytes 208904 | tf_op jit(solution)/shard_map/scatter-add | solution.py:263
  84.8 1.9 %fusion.117 = f32[3,3,131,64]{3,2,1,0:T(8,128)S(1)} fusion(f32[3,3,131,64]{3,2,1,0:T(8,128)S(1)} %fusion.119, s32[]{:T(128)} %bitcast.98, s32[]{:T(128)} %bitcast.99, f32[1,1,9,131,64]{4,3,2,1,0:T(8,128)S(1)} %bitcast.390, pred[]{:T(512)} %and_reduce_fusion), kind=kLoop, calls=%fused_computation.332 | loop fusion | flops 16768 | bytes 208905 | tf_op jit(solution)/shard_map/scatter-add | solution.py:263
  86.9 1.9 %collective-permute-start.8 = (f32[3,1,131,64]{3,2,1,0:T(8,128)S(1)}, f32[3,1,131,64]{3,2,1,0:T(8,128)S(1)}, u32[]{:S(2)}, u32[]{:S(2)}) collective-permute-start(f32[3,1,131,64]{3,2,1,0:T(8,128)S(1)} %get-tuple-element.409), channel_id=1, source_target_pairs={{0,1},{1,2},{2,3},{3,4},{4,5},{5,6},{6,7},{7,8},{8,9},{9,10},{10,1... | collective-permute-start | bytes 301832 | tf_op jit(solution)/shard_map/ppermute | solution.py:35
  88.8 7.6 %collective-permute-start.9 = (f32[3,1,131,64]{3,2,1,0:T(8,128)S(1)}, f32[3,1,131,64]{3,2,1,0:T(8,128)S(1)}, u32[]{:S(2)}, u32[]{:S(2)}) collective-permute-start(f32[3,1,131,64]{3,2,1,0:T(8,128)S(1)} %get-tuple-element.410), channel_id=1, source_target_pairs={{0,15},{1,0},{2,1},{3,2},{4,3},{5,4},{6,5},{7,6},{8,7},{9,8},{10,9... | collective-permute-start | bytes 301832 | tf_op jit(solution)/shard_map/ppermute | solution.py:35
  96.4 7.6 %collective-permute-done.8 = f32[3,1,131,64]{3,2,1,0:T(8,128)S(1)} collective-permute-done((f32[3,1,131,64]{3,2,1,0:T(8,128)S(1)}, f32[3,1,131,64]{3,2,1,0:T(8,128)S(1)}, u32[]{:S(2)}, u32[]{:S(2)}) %collective-permute-start.8) | collective-permute-done | bytes 100640 | tf_op jit(solution)/shard_map/ppermute | solution.py:35
  104.0 0.4 collective-permute-done.9
  104.5 4.8 %collective-permute-start.10 = (bf16[1,1,131,64]{3,2,1,0:T(8,128)(2,1)S(1)}, bf16[1,1,131,64]{3,2,1,0:T(8,128)(2,1)S(1)}, u32[]{:S(2)}, u32[]{:S(2)}) collective-permute-start(bf16[1,1,131,64]{3,2,1,0:T(8,128)(2,1)S(1)} %get-tuple-element.411), channel_id=1, source_target_pairs={{0,16},{16,32},{32,48},{48,64},{64,80},{80,96},{96,112},{112,128},... | collective-permute-start | bytes 50312 | tf_op jit(solution)/shard_map/ppermute | solution.py:35
  109.3 1.9 %collective-permute-start.11 = (bf16[1,1,131,64]{3,2,1,0:T(8,128)(2,1)S(1)}, bf16[1,1,131,64]{3,2,1,0:T(8,128)(2,1)S(1)}, u32[]{:S(2)}, u32[]{:S(2)}) collective-permute-start(bf16[1,1,131,64]{3,2,1,0:T(8,128)(2,1)S(1)} %get-tuple-element.412), channel_id=1, source_target_pairs={{0,496},{16,0},{32,16},{48,32},{64,48},{80,64},{96,80},{112,96},{1... | collective-permute-start | bytes 50312 | tf_op jit(solution)/shard_map/ppermute | solution.py:35
  111.3 0.5 bitcast_multiply_fusion.1
  111.8 4.0 %collective-permute-done.11 = bf16[1,1,131,64]{3,2,1,0:T(8,128)(2,1)S(1)} collective-permute-done((bf16[1,1,131,64]{3,2,1,0:T(8,128)(2,1)S(1)}, bf16[1,1,131,64]{3,2,1,0:T(8,128)(2,1)S(1)}, u32[]{:S(2)}, u32[]{:S(2)}) %collective-permute-start.11) | collective-permute-done | bytes 16800 | tf_op jit(solution)/shard_map/ppermute | solution.py:35
  115.8 0.7 copy.130
  116.6 0.6 copy.129
  (241 shorter events, 12.7 us)
Async XLA Ops:
  0.6 65.6 %copy-start = (bf16[384,128]{1,0:T(8,128)(2,1)S(1)}, bf16[384,128]{1,0:T(8,128)(2,1)}, u32[]{:S(2)}) copy-start(bf16[384,128]{1,0:T(8,128)(2,1)} %param.60) | copy-start | bytes 294916
  0.6 44.3 %copy-start.2 = (f32[3]{0:T(128)S(1)}, f32[3]{0:T(128)}, u32[]{:S(2)}) copy-start(f32[3]{0:T(128)} %constant.553.clone) | copy-start | bytes 40
  0.7 44.3 %copy-start.5 = (f32[3]{0:T(128)S(1)}, f32[3]{0:T(128)}, u32[]{:S(2)}) copy-start(f32[3]{0:T(128)} %constant.560.clone) | copy-start | bytes 40
  0.7 20.2 %collective-permute-start = (f32[1,1,3,64]{3,1,2,0:T(1,128)}, f32[1,1,3,64]{3,1,2,0:T(1,128)S(1)}, u32[]{:S(2)}, u32[]{:S(2)}) collective-permute-start(f32[1,1,3,64]{3,1,2,0:T(1,128)} %param.54), channel_id=1, source_target_pairs={{0,16},{16,32},{32,48},{48,64},{64,80},{80,96},{96,112},{112,128},... | collective-permute-start | bytes 2312 | tf_op jit(solution)/shard_map/ppermute | solution.py:24
  5.8 15.8 %collective-permute-start.1 = (f32[1,1,3,64]{3,1,2,0:T(1,128)}, f32[1,1,3,64]{3,1,2,0:T(1,128)S(1)}, u32[]{:S(2)}, u32[]{:S(2)}) collective-permute-start(f32[1,1,3,64]{3,1,2,0:T(1,128)} %param.54), channel_id=1, source_target_pairs={{16,0},{32,16},{48,32},{64,48},{80,64},{96,80},{112,96},{128,112},... | collective-permute-start | bytes 2312 | tf_op jit(solution)/shard_map/ppermute | solution.py:26
  9.2 43.1 %collective-permute-start.3 = (bf16[1,1,128,64]{2,3,1,0:T(8,128)(2,1)S(1)}, bf16[1,1,128,64]{2,3,1,0:T(8,128)(2,1)S(1)}, u32[]{:S(2)}, u32[]{:S(2)}) collective-permute-start(bf16[1,1,128,64]{2,3,1,0:T(8,128)(2,1)S(1)} %broadcast_multiply_fusion.9), channel_id=1, source_target_pairs={{0,16},{16,32},{32,48},{48,64},{64,80},{80,96},{96,112},{112,128},... | collective-permute-start | bytes 49160 | tf_op jit(solution)/shard_map/ppermute | solution.py:24
  14.1 38.3 %collective-permute-start.4 = (bf16[1,1,128,64]{2,3,1,0:T(8,128)(2,1)S(1)}, bf16[1,1,128,64]{2,3,1,0:T(8,128)(2,1)S(1)}, u32[]{:S(2)}, u32[]{:S(2)}) collective-permute-start(bf16[1,1,128,64]{2,3,1,0:T(8,128)(2,1)S(1)} %broadcast_multiply_fusion.9), channel_id=1, source_target_pairs={{16,0},{32,16},{48,32},{64,48},{80,64},{96,80},{112,96},{128,112},... | collective-permute-start | bytes 49160 | tf_op jit(solution)/shard_map/ppermute | solution.py:26
  21.6 15.5 %collective-permute-start.6 = (f32[3,1,3,64]{3,1,2,0:T(1,128)S(1)}, f32[3,1,3,64]{3,1,2,0:T(1,128)S(1)}, u32[]{:S(2)}, u32[]{:S(2)}) collective-permute-start(f32[3,1,3,64]{3,1,2,0:T(1,128)S(1)} %constant_dynamic-update-slice_fusion), channel_id=1, source_target_pairs={{1,0},{2,1},{3,2},{4,3},{5,4},{6,5},{7,6},{8,7},{9,8},{10,9},{11,1... | collective-permute-start | bytes 6920 | tf_op jit(solution)/shard_map/ppermute | solution.py:26
  35.1 8.6 %collective-permute-start.2 = (f32[3,1,3,64]{3,1,2,0:T(1,128)S(1)}, f32[3,1,3,64]{3,1,2,0:T(1,128)S(1)}, u32[]{:S(2)}, u32[]{:S(2)}) collective-permute-start(f32[3,1,3,64]{3,1,2,0:T(1,128)S(1)} %constant_dynamic-update-slice_fusion), channel_id=1, source_target_pairs={{0,1},{1,2},{2,3},{3,4},{4,5},{5,6},{6,7},{7,8},{8,9},{9,10},{10,1... | collective-permute-start | bytes 6920 | tf_op jit(solution)/shard_map/ppermute | solution.py:24
  44.8 0.7 copy-start.1
  44.8 0.7 copy-start.3
  44.8 0.7 copy-start.4
  44.8 0.7 copy-start.6
  44.8 0.7 copy-start.7
  44.8 0.7 copy-start.8
  52.4 12.4 %collective-permute-start.7 = (bf16[3,1,128,64]{2,3,1,0:T(8,128)(2,1)S(1)}, bf16[3,1,128,64]{2,3,1,0:T(8,128)(2,1)S(1)}, u32[]{:S(2)}, u32[]{:S(2)}) collective-permute-start(bf16[3,1,128,64]{2,3,1,0:T(8,128)(2,1)S(1)} %pad_maximum_fusion.1), channel_id=1, source_target_pairs={{1,0},{2,1},{3,2},{4,3},{5,4},{6,5},{7,6},{8,7},{9,8},{10,9},{11,1... | collective-permute-start | bytes 147464 | tf_op jit(solution)/shard_map/ppermute | solution.py:26
  54.3 9.9 %collective-permute-start.5 = (bf16[3,1,128,64]{2,3,1,0:T(8,128)(2,1)S(1)}, bf16[3,1,128,64]{2,3,1,0:T(8,128)(2,1)S(1)}, u32[]{:S(2)}, u32[]{:S(2)}) collective-permute-start(bf16[3,1,128,64]{2,3,1,0:T(8,128)(2,1)S(1)} %pad_maximum_fusion.1), channel_id=1, source_target_pairs={{0,1},{1,2},{2,3},{3,4},{4,5},{5,6},{6,7},{7,8},{8,9},{9,10},{10,1... | collective-permute-start | bytes 147464 | tf_op jit(solution)/shard_map/ppermute | solution.py:24
  66.0 0.7 copy-start.10
  86.8 24.4 %copy-start.9 = (s32[1,1,64]{2,1,0:T(1,128)S(1)}, s32[1,1,64]{2,1,0:T(1,128)}, u32[]{:S(2)}) copy-start(s32[1,1,64]{2,1,0:T(1,128)} %param.56) | copy-start | bytes 772
  86.9 17.1 %collective-permute-start.8 = (f32[3,1,131,64]{3,2,1,0:T(8,128)S(1)}, f32[3,1,131,64]{3,2,1,0:T(8,128)S(1)}, u32[]{:S(2)}, u32[]{:S(2)}) collective-permute-start(f32[3,1,131,64]{3,2,1,0:T(8,128)S(1)} %get-tuple-element.409), channel_id=1, source_target_pairs={{0,1},{1,2},{2,3},{3,4},{4,5},{5,6},{6,7},{7,8},{8,9},{9,10},{10,1... | collective-permute-start | bytes 301832 | tf_op jit(solution)/shard_map/ppermute | solution.py:35
  88.8 15.6 %collective-permute-start.9 = (f32[3,1,131,64]{3,2,1,0:T(8,128)S(1)}, f32[3,1,131,64]{3,2,1,0:T(8,128)S(1)}, u32[]{:S(2)}, u32[]{:S(2)}) collective-permute-start(f32[3,1,131,64]{3,2,1,0:T(8,128)S(1)} %get-tuple-element.410), channel_id=1, source_target_pairs={{0,15},{1,0},{2,1},{3,2},{4,3},{5,4},{6,5},{7,6},{8,7},{9,8},{10,9... | collective-permute-start | bytes 301832 | tf_op jit(solution)/shard_map/ppermute | solution.py:35
  104.5 7.3 %collective-permute-start.10 = (bf16[1,1,131,64]{3,2,1,0:T(8,128)(2,1)S(1)}, bf16[1,1,131,64]{3,2,1,0:T(8,128)(2,1)S(1)}, u32[]{:S(2)}, u32[]{:S(2)}) collective-permute-start(bf16[1,1,131,64]{3,2,1,0:T(8,128)(2,1)S(1)} %get-tuple-element.411), channel_id=1, source_target_pairs={{0,16},{16,32},{32,48},{48,64},{64,80},{80,96},{96,112},{112,128},... | collective-permute-start | bytes 50312 | tf_op jit(solution)/shard_map/ppermute | solution.py:35
  109.3 6.5 %collective-permute-start.11 = (bf16[1,1,131,64]{3,2,1,0:T(8,128)(2,1)S(1)}, bf16[1,1,131,64]{3,2,1,0:T(8,128)(2,1)S(1)}, u32[]{:S(2)}, u32[]{:S(2)}) collective-permute-start(bf16[1,1,131,64]{3,2,1,0:T(8,128)(2,1)S(1)} %get-tuple-element.412), channel_id=1, source_target_pairs={{0,496},{16,0},{32,16},{48,32},{64,48},{80,64},{96,80},{112,96},{1... | collective-permute-start | bytes 50312 | tf_op jit(solution)/shard_map/ppermute | solution.py:35
where the time goes:
time: 118 us; the launch traced here: 117 us
  starting transfers between devices  50.3 us (43%)
  other arithmetic  24.9 us (21%)
  waiting for transfers between devices  24.4 us (21%)
  matrix products  9.99 us (8%)
  local copies, waits for them, and re-layouts  5.21 us (4%)
  between operations  2.45 us (2%)
    ppermute x4, starting transfers between devices, extended(): lax.ppermute(head, axis, [((i + 1) % count, i) for i in range(count)])  18.6 us
    ppermute x4, starting transfers between devices, shifted(): return lax.ppermute(x, axis, [(i, (i + by) % size) for i in range(size)])  16.2 us
    ppermute x4, starting transfers between devices, extended(): lax.ppermute(tail, axis, [(i, (i + 1) % count) for i in range(count)])  15.4 us
    ppermute x4, waiting for transfers between devices, extended(): lax.ppermute(tail, axis, [(i, (i + 1) % count) for i in range(count)])  12.3 us
    ppermute x4, waiting for transfers between devices, shifted(): return lax.ppermute(x, axis, [(i, (i + by) % size) for i in range(size)])  12 us
    reduce_sum x3, other arithmetic, pair_basis(): math.sqrt(2.0 / CUTOFF) * jnp.sin(orders * math.pi * scaled) / distance  5.71 us
    mul x2, other arithmetic, pair_basis(): math.sqrt(2.0 / CUTOFF) * jnp.sin(orders * math.pi * scaled) / distance  4.06 us
    dot_general x9, matrix products, cell_tail(): jnp.einsum('kic,cj->kij', coeff, near_feat[number], preferred_element_typ...  3.6 us
  transfers between devices with their start and end apart: 12, of which 5 were waited for; matrix products, arithmetic and copies ran while one was open for 15% of the time, Pallas kernels for 0%

commit v1 on v0

v1 whole, which is shorter than its diff:
```python
import math

import jax
import jax.numpy as jnp
from jax import lax
from jax.experimental import pallas as pl
from jax.experimental.pallas import tpu as pltpu
from jax.sharding import PartitionSpec as P

NB = 4
SIDE = 5.0
OFFSETS = ((-1, -1), (-1, 0), (-1, 1), (0, -1), (0, 1), (1, -1), (1, 0), (1, 1))
DEGREE = (0, 1, 1, 1, 2, 2, 2, 2, 2)
S, C, K = 64, 128, 36
LANES = 640
FAR = 1.0e4

SIN_POLY = (0.9999999535014531, -4.934792863930696, 4.058412034401939, -1.331881022938153, 0.21969869886953738)
COS_POLY = (3.1415925800860727, -5.167706881428528, 2.5500314173387735, -0.5980454081793043, 0.07722057976690203)
R3, R5, R15 = math.sqrt(3.0), math.sqrt(5.0), math.sqrt(15.0)
F32, BF16 = jnp.float32, jnp.bfloat16


def poly(coefs, x):
    total = coefs[-1]
    for coef in coefs[-2::-1]:
        total = total * x + coef
    return total


def geometry(centre, other, eye):
    rx, ry, rz = (o - c for o, c in zip(other, centre))
    dist_sq = rx * rx + ry * ry + rz * rz
    if eye is not None:
        dist_sq = dist_sq + eye
    rinv = lax.rsqrt(dist_sq)
    x = jnp.minimum(dist_sq * rinv * (1.0 / SIDE), 1.0)
    y = x - 0.5
    y2 = y * y
    s1 = poly(SIN_POLY, y2)
    c1 = -y * poly(COS_POLY, y2)
    x2 = x * x
    x5 = x2 * x2 * x
    env = 1.0 + x5 * x * (-28.0 + x * (48.0 - 21.0 * x))
    denv = x5 * (-168.0 + x * (336.0 - 168.0 * x))
    norm = math.sqrt(2.0 / SIDE)
    kinv = norm * rinv
    if eye is not None:
        kinv = kinv * (1.0 - eye)
    g = env * kinv
    dg = denv * kinv * (1.0 / SIDE) - g * rinv
    t = 2.0 * c1
    sines = [s1, t * s1]
    cosines = [c1, t * c1 - 1.0]
    for _ in range(NB - 2):
        sines.append(t * sines[-1] - sines[-2])
        cosines.append(t * cosines[-1] - cosines[-2])
    radial = [g * s for s in sines]
    dradial = [dg * s + (g * ((n + 1) * math.pi / SIDE)) * c for n, (s, c) in enumerate(zip(sines, cosines))]
    return radial, dradial, (rx * rinv, ry * rinv, rz * rinv), rinv


def harmonics(u):
    ux, uy, uz = u
    ax, ay, az = R3 * ux, R3 * uy, R3 * uz
    bx, by = R5 * ax, R5 * ay
    return (
        None,
        ax,
        ay,
        az,
        bx * uy,
        by * uz,
        (1.5 * R5) * (uz * uz) - 0.5 * R5,
        bx * uz,
        0.5 * (bx * ux - by * uy),
    )


def kernel(
    nf_h, pos_h, spec_h, occ_h, esh_h, esc_h, rw_h, mix_h, ro_h,
    energy_o, force_o, fgrad_o,
    nf, pos, spec, occ, esh, esc, rw, mix, ro,
    feat, posb, rows, cols, basis, geo, dbs, coeff, pieces, gsend, precv, grecv, giacc,
    ps_sem, pr_sem, fs_sem, fr_sem, ds_sem, dr_sem, gs_sem, gr_sem, in_sem,
):
    sources = (pos_h, occ_h, nf_h, spec_h, esh_h, esc_h, rw_h, mix_h, ro_h)
    targets = (pos, occ, nf, spec, esh, esc, rw, mix, ro)
    loads = [pltpu.make_async_copy(a, b, in_sem.at[i]) for i, (a, b) in enumerate(zip(sources, targets))]
    for load in loads:
        load.start()

    nx, ny = lax.axis_size("gx"), lax.axis_size("gy")
    mx, my = lax.axis_index("gx"), lax.axis_index("gy")

    def device(slot):
        p, q = OFFSETS[slot]
        return (lax.rem(mx + p + nx, nx), lax.rem(my + q + ny, ny))

    def remote(src, dst, send, recv, slot):
        return pltpu.make_async_remote_copy(
            src_ref=src, dst_ref=dst, send_sem=send, recv_sem=recv,
            device_id=device(slot), device_id_type=pl.DeviceIdType.MESH,
        )

    barrier = pltpu.get_barrier_semaphore()
    for slot in range(8):
        pl.semaphore_signal(barrier, inc=1, device_id=device(slot), device_id_type=pl.DeviceIdType.MESH)

    for load in loads[:3]:
        load.wait()
    occ_row = occ[0].astype(F32)
    own = jnp.concatenate([pos[0, a] for a in range(3)] + [occ_row, jnp.zeros((4, S), F32)], axis=0)
    own = jnp.concatenate([own, own], axis=1)
    posb[8] = own
    columns = own.T
    occ_col = columns[0:S, 3:4]
    feat[pl.ds(8 * S, S), :] = nf[0, 0] * occ_col.astype(BF16)
    feat[pl.ds(9 * S, S), :] = jnp.zeros((S, C), BF16)

    pl.semaphore_wait(barrier, 8)
    pos_copies = [remote(posb.at[8], posb.at[7 - s], ps_sem.at[s], pr_sem.at[7 - s], s) for s in range(8)]
    feat_copies = [
        remote(feat.at[pl.ds(8 * S, S)], feat.at[pl.ds((7 - s) * S, S)], fs_sem.at[s], fr_sem.at[7 - s], s)
        for s in range(8)
    ]
    for copy in pos_copies:
        copy.start()
    for copy in feat_copies:
        copy.start()

    for load in loads[3:]:
        load.wait()
    species = spec[0]
    shift_row = jnp.zeros((1, S), F32)
    scale_row = jnp.zeros((1, S), F32)
    for kind in range(esh.shape[0]):
        hit = species == kind
        shift_row = jnp.where(hit, esh[kind], shift_row)
        scale_row = jnp.where(hit, esc[kind], scale_row)
    low = lax.broadcasted_iota(jnp.int32, (1, C), 1) < S
    for a in range(3):
        cols[a] = jnp.broadcast_to(columns[0:S, a : a + 1], (S, C))
    scale_tile = jnp.concatenate([scale_row, jnp.zeros((7, S), F32)], axis=0)
    scale_col = jnp.concatenate([scale_tile, scale_tile], axis=1).T[0:S, 0:1]
    coef_col = occ_col * scale_col

    def pair_tile(tile, own_tile):
        lanes = pl.ds(tile * C, C)

        def body(ib, carry):
            at = pl.ds(pl.multiple_of(ib * 16, 16), 16)
            centre = [cols[a, at, :] for a in range(3)]
            other = [rows[a : a + 1, lanes] for a in range(3)]
            eye = None
            if own_tile:
                sub = lax.broadcasted_iota(jnp.int32, (16, C), 0) + ib * 16
                eye = (sub == lax.broadcasted_iota(jnp.int32, (16, C), 1)).astype(F32)
            radial, dradial, u, rinv = geometry(centre, other, eye)
            for n in range(NB):
                geo[n, at, lanes] = radial[n]
                geo[NB + n, at, lanes] = dradial[n]
            for a in range(3):
                geo[2 * NB + a, at, lanes] = u[a]
            geo[2 * NB + 3, at, lanes] = rinv
            ys = harmonics(u)
            for n in range(NB):
                for lm in range(9):
                    value = radial[n] if lm == 0 else radial[n] * ys[lm]
                    basis[pl.ds(pl.multiple_of((n * 9 + lm) * S + ib * 16, 16), 16), lanes] = value.astype(BF16)
            return carry

        lax.fori_loop(0, 4, body, 0)

    for a in range(3):
        rows[a : a + 1, pl.ds(4 * C, C)] = jnp.where(low, posb[8, a : a + 1, :], FAR)
    pair_tile(4, True)

    for s in range(8):
        pos_copies[s].wait_recv()
    for tile in range(4):
        first, second = OFFSETS[2 * tile], OFFSETS[2 * tile + 1]
        for a in range(3):
            pair = jnp.where(low, posb[2 * tile, a : a + 1, :], posb[2 * tile + 1, a : a + 1, :])
            if a < 2:
                pair = pair + jnp.where(low, SIDE * first[a], SIDE * second[a])
            rows[a : a + 1, pl.ds(tile * C, C)] = pair
        pair_tile(tile, False)

    for s in range(8):
        feat_copies[s].wait_recv()
    sums = jnp.dot(basis[...], feat[...], preferred_element_type=F32)
    weight = [[rw[d, n : n + 1, :] for d in range(3)] for n in range(NB)]
    amp = []
    for lm in range(9):
        total = None
        for n in range(NB):
            k = n * 9 + lm
            term = weight[n][DEGREE[lm]] * sums[k * S : (k + 1) * S]
            total = term if total is None else total + term
        amp.append(total)
    second = amp[1] * amp[1] + amp[2] * amp[2] + amp[3] * amp[3]
    third = amp[4] * amp[4] + amp[5] * amp[5] + amp[6] * amp[6] + amp[7] * amp[7] + amp[8] * amp[8]
    invariants = jnp.concatenate([amp[0].astype(BF16), second.astype(BF16), third.astype(BF16)], axis=1)
    pre = jnp.dot(invariants, mix[...], preferred_element_type=F32)
    sigma = jax.nn.sigmoid(pre)
    readout = ro[...]
    dpre = (coef_col * readout * sigma * (1.0 + pre * (1.0 - sigma))).astype(BF16)
    dinv = lax.dot_general(dpre, mix[...], (((1,), (1,)), ((), ())), preferred_element_type=F32)
    for lm in range(9):
        d = DEGREE[lm]
        damp = dinv[:, d * C : (d + 1) * C]
        if d > 0:
            damp = 2.0 * amp[lm] * damp
        for n in range(NB):
            coeff[pl.ds((n * 9 + lm) * S, S), :] = (weight[n][d] * damp).astype(BF16)

    piece_copies = []
    for half in range(2):
        part = lax.dot_general(
            coeff[...], basis[:, pl.ds(half * 2 * C, 2 * C)], (((0,), (0,)), ((), ())), preferred_element_type=F32
        ).T.astype(BF16)
        for i in range(4):
            s = half * 4 + i
            pieces[s] = part[i * S : (i + 1) * S]
            copy = remote(pieces.at[s], precv.at[7 - s], ds_sem.at[s], dr_sem.at[7 - s], s)
            copy.start()
            piece_copies.append(copy)
    own_part = lax.dot_general(
        coeff[...], basis[:, pl.ds(4 * C, C)], (((0,), (0,)), ((), ())), preferred_element_type=F32
    )

    energy_row = jnp.sum((pre * sigma * readout).T, axis=0, keepdims=True)
    energy_o[0] = occ_row * (shift_row + scale_row * energy_row)

    def force_tile(tile, column):
        lanes = pl.ds(tile * C, C)

        def body(ib, carry):
            at = pl.ds(pl.multiple_of(ib * 16, 16), 16)
            radial = [geo[n, at, lanes] for n in range(NB)]
            dradial = [geo[NB + n, at, lanes] for n in range(NB)]
            u = [geo[2 * NB + a, at, lanes] for a in range(3)]
            rinv = geo[2 * NB + 3, at, lanes]
            ys = harmonics(u)
            along = [None] * NB
            across = [None] * 9
            for n in range(NB):
                for lm in range(9):
                    value = dbs[pl.ds(pl.multiple_of((n * 9 + lm) * S + ib * 16, 16), 16), pl.ds(column, C)]
                    term = value if lm == 0 else value * ys[lm]
                    along[n] = term if along[n] is None else along[n] + term
                    if lm:
                        term = radial[n] * value
                        across[lm] = term if across[lm] is None else across[lm] + term
            outward = along[0] * dradial[0]
            for n in range(1, NB):
                outward = outward + along[n] * dradial[n]
            e = across
            ux, uy, uz = u
            vx = R3 * e[1] + R15 * (uy * e[4] + uz * e[7] + ux * e[8])
            vy = R3 * e[2] + R15 * (ux * e[4] + uz * e[5] - uy * e[8])
            vz = R3 * e[3] + R15 * (uy * e[5] + ux * e[7]) + (3.0 * R5) * (uz * e[6])
            radial_part = outward - rinv * (ux * vx + uy * vy + uz * vz)
            sums_j = []
            for a, v in enumerate((vx, vy, vz)):
                grad = rinv * v + u[a] * radial_part
                if tile == 0:
                    giacc[a, at, :] = grad
                else:
                    giacc[a, at, :] = giacc[a, at, :] + grad
                sums_j.append(carry[a] + grad[0:8] + grad[8:16])
            return tuple(sums_j)

        zero = jnp.zeros((8, C), F32)
        totals = lax.fori_loop(0, 4, body, (zero, zero, zero))
        return jnp.concatenate(
            [jnp.sum(t, axis=0, keepdims=True) for t in totals] + [jnp.zeros((5, C), F32)], axis=0
        )

    grad_copies = []
    for half in range(2):
        dbs[...] = lax.dot_general(
            coeff[...], feat[pl.ds(half * 4 * S, 4 * S), :], (((1,), (1,)), ((), ())), preferred_element_type=F32
        )
        for i in range(2):
            tile = half * 2 + i
            gsend[tile] = force_tile(tile, i * C)
            for s in (2 * tile, 2 * tile + 1):
                copy = remote(gsend.at[tile], grecv.at[7 - s], gs_sem.at[s], gr_sem.at[7 - s], s)
                copy.start()
                grad_copies.append(copy)
    dbs[:, pl.ds(0, C)] = lax.dot_general(
        coeff[...], feat[pl.ds(8 * S, 2 * S), :], (((1,), (1,)), ((), ())), preferred_element_type=F32
    )
    own_grad = force_tile(4, 0)
    centre_rows = [jnp.sum(giacc[a].T, axis=0, keepdims=True) for a in range(3)]

    for s in range(8):
        piece_copies[s].wait_recv()
    gathered = precv[0].astype(F32)
    for s in range(1, 8):
        gathered = gathered + precv[s].astype(F32)
    fgrad_o[0, 0] = (gathered + own_part.T[:S, :]) * occ_col

    for s in range(8):
        grad_copies[s].wait_recv()
    upper = grecv[0] + grecv[2] + grecv[4] + grecv[6]
    lower = grecv[1] + grecv[3] + grecv[5] + grecv[7] + own_grad
    back = lower[0:3, 0:S] + upper[0:3, S:C]
    for a in range(3):
        force_o[0, a] = centre_rows[a] - back[a : a + 1]

    for copies in (pos_copies, feat_copies, piece_copies, grad_copies):
        for copy in copies:
            copy.wait_send()


def emit(a, b, c, ao, bo, co, sem):
    copies = [pltpu.make_async_copy(x, y, sem.at[i]) for i, (x, y) in enumerate(((a, ao), (b, bo), (c, co)))]
    for copy in copies:
        copy.start()
    for copy in copies:
        copy.wait()


def shards(nf, pos, spec, occ, esh, esc, rw, mix, ro):
    vmem = pl.BlockSpec(memory_space=pltpu.VMEM)
    hbm = pl.BlockSpec(memory_space=pltpu.HBM)
    dma = pltpu.SemaphoreType.DMA((8,))
    shapes = (
        jax.ShapeDtypeStruct((1, 1, S), F32),
        jax.ShapeDtypeStruct((1, 3, 1, S), F32),
        jax.ShapeDtypeStruct((1, 1, S, C), F32),
    )
    inputs = (nf.swapaxes(2, 3), pos.swapaxes(1, 2), spec, occ, esh, esc, rw.swapaxes(0, 1), mix, ro.reshape(1, C))
    results = pl.pallas_call(
        kernel,
        out_shape=shapes,
        in_specs=[hbm] * 9,
        out_specs=(vmem, vmem, vmem),
        scratch_shapes=[
            pltpu.VMEM((1, 1, S, C), BF16),
            pltpu.VMEM((1, 3, 1, S), F32),
            pltpu.VMEM((1, 1, S), jnp.int32),
            pltpu.VMEM((1, 1, S), jnp.int32),
            pltpu.SMEM(esh.shape, F32),
            pltpu.SMEM(esh.shape, F32),
            pltpu.VMEM((3, NB, C), F32),
            pltpu.VMEM((3 * C, C), BF16),
            pltpu.VMEM((1, C), F32),
            pltpu.VMEM((LANES, C), BF16),
            pltpu.VMEM((9, 8, C), F32),
            pltpu.VMEM((8, LANES), F32),
            pltpu.VMEM((3, S, C), F32),
            pltpu.VMEM((K * S, LANES), BF16),
            pltpu.VMEM((3 * NB, S, LANES), F32),
            pltpu.VMEM((K * S, 2 * C), F32),
            pltpu.VMEM((K * S, C), BF16),
            pltpu.VMEM((8, S, C), BF16),
            pltpu.VMEM((4, 8, C), F32),
            pltpu.VMEM((8, S, C), BF16),
            pltpu.VMEM((8, 8, C), F32),
            pltpu.VMEM((3, S, C), F32),
            dma, dma, dma, dma, dma, dma, dma, dma,
            pltpu.SemaphoreType.DMA((9,)),
        ],
        compiler_params=pltpu.CompilerParams(
            collective_id=0, has_side_effects=True, vmem_limit_bytes=48 * 1024 * 1024
        ),
        cost_estimate=pl.CostEstimate(flops=1_100_000_000, bytes_accessed=400_000, transcendentals=100_000),
    )(*[pltpu.with_memory_space_constraint(v, pltpu.HBM) for v in inputs])
    energy, forces, fgrad = pl.pallas_call(
        emit,
        out_shape=shapes,
        in_specs=[vmem] * 3,
        out_specs=(hbm,) * 3,
        scratch_shapes=[pltpu.SemaphoreType.DMA((3,))],
    )(*results)
    return energy, forces.swapaxes(1, 2), fgrad.swapaxes(2, 3)


def solution(mesh):
    placed = (
        P("gx", "gy", None, None),
        P("gx", "gy", None, None),
        P("gx", "gy", None),
        P("gx", "gy", None),
        P(), P(), P(), P(), P(),
    )
    return jax.shard_map(
        shards,
        mesh=mesh,
        in_specs=placed,
        out_specs=(P("gx", "gy", None), P("gx", "gy", None, None), P("gx", "gy", None, None)),
        check_vma=False,
    )
```

time: 118 us -> 37.4 us (0.32)
  the two profiles are of different devices: /device:TPU:25 before, /device:TPU:1 now
where the time goes in v1:
time: 37.4 us; the launch traced here: 37.1 us
  Pallas kernels  34.8 us (93%)
  local copies, waits for them, and re-layouts  1.69 us (5%)
  between operations  0.65 us (2%)
    pallas_call x1, Pallas kernels, shards(): pl.pallas_call(kernel, out_shape=shapes, in_specs=[hbm] * 9, out_specs=(v...  33.4 us
    unnamed x6, local copies, waits for them, and re-layouts  1.69 us
    pallas_call x1, Pallas kernels, shards(): pl.pallas_call(emit, out_shape=shapes, in_specs=[vmem] * 3, out_specs=(hb...  1.41 us

profile of v1, /device:TPU:1, one launch (start us, length us, event | category | flops | bytes accessed | tf_op | source)
XLA Modules:
  0.0 37.1 jit_solution(17869687838525484930)
XLA Ops:
  0.6 33.4 %shard_map.112 = (f32[1,1,64]{2,1,0:T(1,128)S(1)}, f32[1,3,1,64]{3,2,1,0:T(1,128)S(1)}, f32[1,1,64,128]{3,2,1,0:T(8,128)S(1)}) custom-call(bf16[1,1,64,128]{3,2,1,0:T(8,128)(2,1)} %bitcast.9, f32[1,3,1,64]{3,2,1,0:T(1,128)} %bitcast.11, s32[1,1,64]{2,1,0:T(1,128)} %spec_h.1, s32[1,1,64]{2,1,0:T(1,128)} %occ_h.1, f32[10]{0:T(128)} %esh_h.1, f32[10]{0:T(128)} %esc_h.1, ...), custom_call_target="tpu_custom_call" | custom-call | flops 1100000000 | bytes 400000 | tf_op jit(solution)/shard_map/pallas_call | solution.py:337
  34.0 0.0 copy-start
  34.0 0.6 %copy-done = f32[1,1,64,128]{3,2,1,0:T(8,128)} copy-done((f32[1,1,64,128]{3,2,1,0:T(8,128)}, f32[1,1,64,128]{3,2,1,0:T(8,128)S(1)}, u32[]{:S(2)}) %copy-start) | copy-done | bytes 32792
  34.6 0.0 copy-start.2
  34.6 0.5 %copy-done.2 = f32[1,1,64]{2,1,0:T(1,128)} copy-done((f32[1,1,64]{2,1,0:T(1,128)}, f32[1,1,64]{2,1,0:T(1,128)S(1)}, u32[]{:S(2)}) %copy-start.2) | copy-done | bytes 280
  35.1 0.0 copy-start.1
  35.1 0.6 %copy-done.1 = f32[1,3,1,64]{3,2,1,0:T(1,128)} copy-done((f32[1,3,1,64]{3,2,1,0:T(1,128)}, f32[1,3,1,64]{3,2,1,0:T(1,128)S(1)}, u32[]{:S(2)}) %copy-start.1) | copy-done | bytes 792
  35.7 1.4 %shard_map.113 = (f32[1,1,64]{2,1,0:T(1,128)}, f32[1,3,1,64]{3,2,1,0:T(1,128)}, f32[1,1,64,128]{3,2,1,0:T(8,128)}) custom-call(f32[1,1,64]{2,1,0:T(1,128)} %copy-done.2, f32[1,3,1,64]{3,2,1,0:T(1,128)} %copy-done.1, f32[1,1,64,128]{3,2,1,0:T(8,128)} %copy-done), custom_call_target="tpu_custom_call" | custom-call | tf_op jit(solution)/shard_map/pallas_call | solution.py:373
Async XLA Ops:
  34.0 0.6 %copy-start = (f32[1,1,64,128]{3,2,1,0:T(8,128)}, f32[1,1,64,128]{3,2,1,0:T(8,128)S(1)}, u32[]{:S(2)}) copy-start(f32[1,1,64,128]{3,2,1,0:T(8,128)S(1)} %get-tuple-element.11.c) | copy-start | bytes 98308
  34.6 0.5 %copy-start.2 = (f32[1,1,64]{2,1,0:T(1,128)}, f32[1,1,64]{2,1,0:T(1,128)S(1)}, u32[]{:S(2)}) copy-start(f32[1,1,64]{2,1,0:T(1,128)S(1)} %get-tuple-element.9.a) | copy-start | bytes 772
  35.1 0.6 %copy-start.1 = (f32[1,3,1,64]{3,2,1,0:T(1,128)}, f32[1,3,1,64]{3,2,1,0:T(1,128)S(1)}, u32[]{:S(2)}) copy-start(f32[1,3,1,64]{3,2,1,0:T(1,128)S(1)} %get-tuple-element.10.b) | copy-start | bytes 2308

commit v2 on v1

--- a/solution.py
+++ b/solution.py
@@ -9,7 +9,9 @@
 
 NB = 4
 SIDE = 5.0
-OFFSETS = ((-1, -1), (-1, 0), (-1, 1), (0, -1), (0, 1), (1, -1), (1, 0), (1, 1))
+OFFSETS = ((-1, 1), (1, 1), (0, 1), (1, 0), (-1, -1), (1, -1), (0, -1), (-1, 0))
+OPPOSITE = (5, 4, 6, 7, 1, 0, 2, 3)
+MIRROR = (1, 0, 2, 7, 5, 4, 6, 3)
 DEGREE = (0, 1, 1, 1, 2, 2, 2, 2, 2)
 S, C, K = 64, 128, 36
 LANES = 640
@@ -81,31 +83,44 @@
     nf_h, pos_h, spec_h, occ_h, esh_h, esc_h, rw_h, mix_h, ro_h,
     energy_o, force_o, fgrad_o,
     nf, pos, spec, occ, esh, esc, rw, mix, ro,
-    feat, posb, rows, cols, basis, geo, dbs, coeff, pieces, gsend, precv, grecv, giacc,
+    feat, posb, rows, cols, basis, geo, dbs, coeff, coeff_t, near, pieces, gsend, precv, grecv, giacc,
     ps_sem, pr_sem, fs_sem, fr_sem, ds_sem, dr_sem, gs_sem, gr_sem, in_sem,
 ):
+    nx, ny = lax.axis_size("gx"), lax.axis_size("gy")
+    mx, my = lax.axis_index("gx"), lax.axis_index("gy")
+
+    inner = lax.div(my + ny - 1, ny)
+    flip = 2 * inner - 1
+
+    def device(slot):
+        p, q = OFFSETS[slot]
+        return (lax.rem(mx + p + nx, nx), lax.rem(my + q * flip + ny, ny))
+
+    def landing(slot):
+        if OFFSETS[slot][1] == 0:
+            return OPPOSITE[slot]
+        other = lax.div(device(slot)[1] + ny - 1, ny)
+        mixed = inner + other - 2 * inner * other
+        return OPPOSITE[slot] + mixed * (MIRROR[slot] - OPPOSITE[slot])
+
+    target = [landing(s) for s in range(8)]
+
+    def remote(src, dst, send, recv, slot):
+        return pltpu.make_async_remote_copy(
+            src_ref=src, dst_ref=dst, send_sem=send, recv_sem=recv,
+            device_id=device(slot), device_id_type=pl.DeviceIdType.MESH,
+        )
+
+    barrier = pltpu.get_barrier_semaphore()
+    for slot in range(8):
+        pl.semaphore_signal(barrier, inc=1, device_id=device(slot), device_id_type=pl.DeviceIdType.MESH)
+
     sources = (pos_h, occ_h, nf_h, spec_h, esh_h, esc_h, rw_h, mix_h, ro_h)
     targets = (pos, occ, nf, spec, esh, esc, rw, mix, ro)
     loads = [pltpu.make_async_copy(a, b, in_sem.at[i]) for i, (a, b) in enumerate(zip(sources, targets))]
     for load in loads:
         load.start()
 
-    nx, ny = lax.axis_size("gx"), lax.axis_size("gy")
-    mx, my = lax.axis_index("gx"), lax.axis_index("gy")
-
-    def device(slot):
-        p, q = OFFSETS[slot]
-        return (lax.rem(mx + p + nx, nx), lax.rem(my + q + ny, ny))
-
-    def remote(src, dst, send, recv, slot):
-        return pltpu.make_async_remote_copy(
-            src_ref=src, dst_ref=dst, send_sem=send, recv_sem=recv,
-            device_id=device(slot), device_id_type=pl.DeviceIdType.MESH,
-        )
-
-    barrier = pltpu.get_barrier_semaphore()
-    for slot in range(8):
-        pl.semaphore_signal(barrier, inc=1, device_id=device(slot), device_id_type=pl.DeviceIdType.MESH)
 
     for load in loads[:3]:
         load.wait()
@@ -115,19 +130,27 @@
     posb[8] = own
     columns = own.T
     occ_col = columns[0:S, 3:4]
-    feat[pl.ds(8 * S, S), :] = nf[0, 0] * occ_col.astype(BF16)
-    feat[pl.ds(9 * S, S), :] = jnp.zeros((S, C), BF16)
+    feat[8] = nf[0, 0] * occ_col.astype(BF16)
+    feat[9] = jnp.zeros((S, C), BF16)
 
     pl.semaphore_wait(barrier, 8)
-    pos_copies = [remote(posb.at[8], posb.at[7 - s], ps_sem.at[s], pr_sem.at[7 - s], s) for s in range(8)]
-    feat_copies = [
-        remote(feat.at[pl.ds(8 * S, S)], feat.at[pl.ds((7 - s) * S, S)], fs_sem.at[s], fr_sem.at[7 - s], s)
-        for s in range(8)
-    ]
-    for copy in pos_copies:
-        copy.start()
-    for copy in feat_copies:
-        copy.start()
+    def pos_copy(s, there):
+        return remote(posb.at[8], posb.at[there], ps_sem.at[s], pr_sem.at[there], s)
+
+    def feat_copy(s, there):
+        return remote(feat.at[8], feat.at[there], fs_sem.at[s], fr_sem.at[there], s)
+
+    def piece_copy(s, there):
+        return remote(pieces.at[s], precv.at[there], ds_sem.at[s], dr_sem.at[there], s)
+
+    def grad_copy(s, there):
+        return remote(gsend.at[s // 2], grecv.at[there], gs_sem.at[s], gr_sem.at[there], s)
+
+    for group in (range(3), range(3, 8)):
+        for s in group:
+            pos_copy(s, target[s]).start()
+        for s in group:
+            feat_copy(s, target[s]).start()
 
     for load in loads[3:]:
         load.wait()
@@ -170,26 +193,39 @@
                     basis[pl.ds(pl.multiple_of((n * 9 + lm) * S + ib * 16, 16), 16), lanes] = value.astype(BF16)
             return carry
 
-        lax.fori_loop(0, 4, body, 0)
+        lax.fori_loop(0, 4, body, 0, unroll=True)
 
     for a in range(3):
         rows[a : a + 1, pl.ds(4 * C, C)] = jnp.where(low, posb[8, a : a + 1, :], FAR)
     pair_tile(4, True)
 
-    for s in range(8):
-        pos_copies[s].wait_recv()
-    for tile in range(4):
+    def neighbour_tile(tile):
+        for s in (2 * tile, 2 * tile + 1):
+            pos_copy(s, s).wait_recv()
         first, second = OFFSETS[2 * tile], OFFSETS[2 * tile + 1]
         for a in range(3):
             pair = jnp.where(low, posb[2 * tile, a : a + 1, :], posb[2 * tile + 1, a : a + 1, :])
-            if a < 2:
-                pair = pair + jnp.where(low, SIDE * first[a], SIDE * second[a])
+            if a == 0:
+                pair = pair + jnp.where(low, SIDE * first[0], SIDE * second[0])
+            if a == 1:
+                pair = pair + jnp.where(low, SIDE * first[1], SIDE * second[1]) * flip.astype(F32)
             rows[a : a + 1, pl.ds(tile * C, C)] = pair
         pair_tile(tile, False)
 
-    for s in range(8):
-        feat_copies[s].wait_recv()
-    sums = jnp.dot(basis[...], feat[...], preferred_element_type=F32)
+    neighbour_tile(3)
+    neighbour_tile(2)
+    for s in (7, 6, 5, 4):
+        feat_copy(s, s).wait_recv()
+    near[...] = jnp.dot(
+        basis[:, pl.ds(2 * C, 3 * C)], feat[4:10].reshape(6 * S, C), preferred_element_type=F32
+    )
+    neighbour_tile(1)
+    neighbour_tile(0)
+    for s in (3, 2, 1, 0):
+        feat_copy(s, s).wait_recv()
+    sums = near[...] + jnp.dot(
+        basis[:, pl.ds(0, 2 * C)], feat[0:4].reshape(4 * S, C), preferred_element_type=F32
+    )
     weight = [[rw[d, n : n + 1, :] for d in range(3)] for n in range(NB)]
     amp = []
     for lm in range(9):
@@ -214,24 +250,8 @@
             damp = 2.0 * amp[lm] * damp
         for n in range(NB):
             coeff[pl.ds((n * 9 + lm) * S, S), :] = (weight[n][d] * damp).astype(BF16)
-
-    piece_copies = []
-    for half in range(2):
-        part = lax.dot_general(
-            coeff[...], basis[:, pl.ds(half * 2 * C, 2 * C)], (((0,), (0,)), ((), ())), preferred_element_type=F32
-        ).T.astype(BF16)
-        for i in range(4):
-            s = half * 4 + i
-            pieces[s] = part[i * S : (i + 1) * S]
-            copy = remote(pieces.at[s], precv.at[7 - s], ds_sem.at[s], dr_sem.at[7 - s], s)
-            copy.start()
-            piece_copies.append(copy)
-    own_part = lax.dot_general(
-        coeff[...], basis[:, pl.ds(4 * C, C)], (((0,), (0,)), ((), ())), preferred_element_type=F32
-    )
-
-    energy_row = jnp.sum((pre * sigma * readout).T, axis=0, keepdims=True)
-    energy_o[0] = occ_row * (shift_row + scale_row * energy_row)
+    for k in range(K // 2):
+        coeff_t[:, pl.ds(k * C, C)] = coeff[pl.ds(k * C, C), :].T
 
     def force_tile(tile, column):
         lanes = pl.ds(tile * C, C)
@@ -273,47 +293,55 @@
             return tuple(sums_j)
 
         zero = jnp.zeros((8, C), F32)
-        totals = lax.fori_loop(0, 4, body, (zero, zero, zero))
+        totals = lax.fori_loop(0, 4, body, (zero, zero, zero), unroll=True)
         return jnp.concatenate(
             [jnp.sum(t, axis=0, keepdims=True) for t in totals] + [jnp.zeros((5, C), F32)], axis=0
         )
 
-    grad_copies = []
+    def feature_part(lanes):
+        return jnp.dot(coeff_t[...], basis[:, lanes], preferred_element_type=F32).T
+
     for half in range(2):
         dbs[...] = lax.dot_general(
-            coeff[...], feat[pl.ds(half * 4 * S, 4 * S), :], (((1,), (1,)), ((), ())), preferred_element_type=F32
+            coeff[...], feat[half * 4 : half * 4 + 4].reshape(4 * S, C), (((1,), (1,)), ((), ())), preferred_element_type=F32
         )
+        part = feature_part(pl.ds(half * 2 * C, 2 * C)).astype(BF16)
+        for i in range(4):
+            s = half * 4 + i
+            pieces[s] = part[i * S : (i + 1) * S]
+            piece_copy(s, target[s]).start()
         for i in range(2):
             tile = half * 2 + i
             gsend[tile] = force_tile(tile, i * C)
             for s in (2 * tile, 2 * tile + 1):
-                copy = remote(gsend.at[tile], grecv.at[7 - s], gs_sem.at[s], gr_sem.at[7 - s], s)
-                copy.start()
-                grad_copies.append(copy)
+                grad_copy(s, target[s]).start()
+
+    own_part = feature_part(pl.ds(4 * C, C))
     dbs[:, pl.ds(0, C)] = lax.dot_general(
-        coeff[...], feat[pl.ds(8 * S, 2 * S), :], (((1,), (1,)), ((), ())), preferred_element_type=F32
+        coeff[...], feat[8:10].reshape(2 * S, C), (((1,), (1,)), ((), ())), preferred_element_type=F32
     )
     own_grad = force_tile(4, 0)
     centre_rows = [jnp.sum(giacc[a].T, axis=0, keepdims=True) for a in range(3)]
+    energy_row = jnp.sum((pre * sigma * readout).T, axis=0, keepdims=True)
+    energy_o[0] = occ_row * (shift_row + scale_row * energy_row)
+
+    gathered = own_part[:S, :]
+    for s in (7, 6, 5, 4, 3, 2, 1, 0):
+        piece_copy(s, s).wait_recv()
+        gathered = gathered + precv[s].astype(F32)
+    fgrad_o[0, 0] = gathered * occ_col
 
     for s in range(8):
-        piece_copies[s].wait_recv()
-    gathered = precv[0].astype(F32)
-    for s in range(1, 8):
-        gathered = gathered + precv[s].astype(F32)
-    fgrad_o[0, 0] = (gathered + own_part.T[:S, :]) * occ_col
-
-    for s in range(8):
-        grad_copies[s].wait_recv()
-    upper = grecv[0] + grecv[2] + grecv[4] + grecv[6]
-    lower = grecv[1] + grecv[3] + grecv[5] + grecv[7] + own_grad
+        grad_copy(s, s).wait_recv()
+    upper = grecv[0] + grecv[3] + grecv[4] + grecv[7]
+    lower = grecv[1] + grecv[2] + grecv[5] + grecv[6] + own_grad
     back = lower[0:3, 0:S] + upper[0:3, S:C]
     for a in range(3):
         force_o[0, a] = centre_rows[a] - back[a : a + 1]
 
-    for copies in (pos_copies, feat_copies, piece_copies, grad_copies):
-        for copy in copies:
-            copy.wait_send()
+    for s in range(8):
+        for copy in (pos_copy, feat_copy, piece_copy, grad_copy):
+            copy(s, target[s]).wait_send()
 
 
 def emit(a, b, c, ao, bo, co, sem):
@@ -349,7 +377,7 @@
             pltpu.VMEM((3, NB, C), F32),
             pltpu.VMEM((3 * C, C), BF16),
             pltpu.VMEM((1, C), F32),
-            pltpu.VMEM((LANES, C), BF16),
+            pltpu.VMEM((10, S, C), BF16),
             pltpu.VMEM((9, 8, C), F32),
             pltpu.VMEM((8, LANES), F32),
             pltpu.VMEM((3, S, C), F32),
@@ -357,6 +385,8 @@
             pltpu.VMEM((3 * NB, S, LANES), F32),
             pltpu.VMEM((K * S, 2 * C), F32),
             pltpu.VMEM((K * S, C), BF16),
+            pltpu.VMEM((C, K * S), BF16),
+            pltpu.VMEM((K * S, C), F32),
             pltpu.VMEM((8, S, C), BF16),
             pltpu.VMEM((4, 8, C), F32),
             pltpu.VMEM((8, S, C), BF16),
@@ -376,6 +406,7 @@
         in_specs=[vmem] * 3,
         out_specs=(hbm,) * 3,
         scratch_shapes=[pltpu.SemaphoreType.DMA((3,))],
+        compiler_params=pltpu.CompilerParams(vmem_limit_bytes=1024 * 1024),
     )(*results)
     return energy, forces.swapaxes(1, 2), fgrad.swapaxes(2, 3)
 

time: 37.4 us -> 30.5 us (0.82)
  Pallas kernels: 34.8 us -> 29.7 us
  local copies, waits for them, and re-layouts: 1.69 us -> 0 us
    pallas_call x1, Pallas kernels: 33.4 us -> 29.1 us  [shards(): pl.pallas_call(kernel, out_shape=shapes, in_specs=[hbm] * 9, out_specs=(v...]
    unnamed x6 -> x0, local copies, waits for them, and re-layouts: 1.69 us -> none
    pallas_call x1, Pallas kernels: 1.41 us -> 0.65 us  [shards(): pl.pallas_call(emit, out_shape=shapes, in_specs=[vmem] * 3, out_specs=(hb...]
where the time goes in v2:
time: 30.5 us; the launch traced here: 30.4 us
  Pallas kernels  29.7 us (97%)
  between operations  0.64 us (2%)
    pallas_call x1, Pallas kernels, shards(): pl.pallas_call(kernel, out_shape=shapes, in_specs=[hbm] * 9, out_specs=(v...  29.1 us
    pallas_call x1, Pallas kernels, shards(): pl.pallas_call(emit, out_shape=shapes, in_specs=[vmem] * 3, out_specs=(hb...  0.65 us

profile of v2, /device:TPU:1, one launch (start us, length us, event | category | flops | bytes accessed | tf_op | source)
XLA Modules:
  0.0 30.4 jit_solution(7900072639547213293)
XLA Ops:
  0.6 29.1 %shard_map.112 = (f32[1,1,64]{2,1,0:T(1,128)S(1)}, f32[1,3,1,64]{3,2,1,0:T(1,128)S(1)}, f32[1,1,64,128]{3,2,1,0:T(8,128)S(1)}) custom-call(bf16[1,1,64,128]{3,2,1,0:T(8,128)(2,1)} %bitcast.9, f32[1,3,1,64]{3,2,1,0:T(1,128)} %bitcast.11, s32[1,1,64]{2,1,0:T(1,128)} %spec_h.1, s32[1,1,64]{2,1,0:T(1,128)} %occ_h.1, f32[10]{0:T(128)} %esh_h.1, f32[10]{0:T(128)} %esc_h.1, ...), custom_call_target="tpu_custom_call" | custom-call | flops 1100000000 | bytes 400000 | tf_op jit(solution)/shard_map/pallas_call | solution.py:365
  29.7 0.7 %shard_map.113 = (f32[1,1,64]{2,1,0:T(1,128)}, f32[1,3,1,64]{3,2,1,0:T(1,128)}, f32[1,1,64,128]{3,2,1,0:T(8,128)}) custom-call(f32[1,1,64]{2,1,0:T(1,128)S(1)} %get-tuple-element.9.a, f32[1,3,1,64]{3,2,1,0:T(1,128)S(1)} %get-tuple-element.10.b, f32[1,1,64,128]{3,2,1,0:T(8,128)S(1)} %get-tuple-element.11.c), custom_call_target="tpu_custom_call" | custom-call | tf_op jit(solution)/shard_map/pallas_call | solution.py:403

commit v3 on v2

--- a/solution.py
+++ b/solution.py
@@ -89,19 +89,23 @@
     nx, ny = lax.axis_size("gx"), lax.axis_size("gy")
     mx, my = lax.axis_index("gx"), lax.axis_index("gy")
 
-    inner = lax.div(my + ny - 1, ny)
-    flip = 2 * inner - 1
+    def wrapped(index, step, count):
+        index = index + step
+        index = jnp.where(index < 0, index + count, index)
+        return jnp.where(index >= count, index - count, index)
+
+    first_column = my == 0
+    flip = jnp.where(first_column, -1, 1)
 
     def device(slot):
         p, q = OFFSETS[slot]
-        return (lax.rem(mx + p + nx, nx), lax.rem(my + q * flip + ny, ny))
+        return (wrapped(mx, p, nx) if p else mx, wrapped(my, q * flip, ny) if q else my)
 
     def landing(slot):
         if OFFSETS[slot][1] == 0:
             return OPPOSITE[slot]
-        other = lax.div(device(slot)[1] + ny - 1, ny)
-        mixed = inner + other - 2 * inner * other
-        return OPPOSITE[slot] + mixed * (MIRROR[slot] - OPPOSITE[slot])
+        mixed = jnp.logical_xor(first_column, device(slot)[1] == 0)
+        return jnp.where(mixed, MIRROR[slot], OPPOSITE[slot])
 
     target = [landing(s) for s in range(8)]
 
@@ -299,13 +303,13 @@
         )
 
     def feature_part(lanes):
-        return jnp.dot(coeff_t[...], basis[:, lanes], preferred_element_type=F32).T
+        return jnp.dot(coeff_t[...], basis[:, lanes], preferred_element_type=F32)
 
     for half in range(2):
         dbs[...] = lax.dot_general(
             coeff[...], feat[half * 4 : half * 4 + 4].reshape(4 * S, C), (((1,), (1,)), ((), ())), preferred_element_type=F32
         )
-        part = feature_part(pl.ds(half * 2 * C, 2 * C)).astype(BF16)
+        part = feature_part(pl.ds(half * 2 * C, 2 * C)).astype(BF16).T
         for i in range(4):
             s = half * 4 + i
             pieces[s] = part[i * S : (i + 1) * S]
@@ -316,7 +320,7 @@
             for s in (2 * tile, 2 * tile + 1):
                 grad_copy(s, target[s]).start()
 
-    own_part = feature_part(pl.ds(4 * C, C))
+    own_part = feature_part(pl.ds(4 * C, C)).T
     dbs[:, pl.ds(0, C)] = lax.dot_general(
         coeff[...], feat[8:10].reshape(2 * S, C), (((1,), (1,)), ((), ())), preferred_element_type=F32
     )

time: 30.5 us -> 30.5 us (level)
  no operation moved by 1% of the time
where the time goes in v3:
time: 30.5 us; the launch traced here: 30.4 us
  Pallas kernels  29.7 us (97%)
  between operations  0.64 us (2%)
    pallas_call x1, Pallas kernels, shards(): pl.pallas_call(kernel, out_shape=shapes, in_specs=[hbm] * 9, out_specs=(v...  29.1 us
    pallas_call x1, Pallas kernels, shards(): pl.pallas_call(emit, out_shape=shapes, in_specs=[vmem] * 3, out_specs=(hb...  0.65 us

profile of v3, /device:TPU:1, one launch (start us, length us, event | category | flops | bytes accessed | tf_op | source)
XLA Modules:
  0.0 30.4 jit_solution(6656910536439327805)
XLA Ops:
  0.6 29.1 %shard_map.112 = (f32[1,1,64]{2,1,0:T(1,128)S(1)}, f32[1,3,1,64]{3,2,1,0:T(1,128)S(1)}, f32[1,1,64,128]{3,2,1,0:T(8,128)S(1)}) custom-call(bf16[1,1,64,128]{3,2,1,0:T(8,128)(2,1)} %bitcast.9, f32[1,3,1,64]{3,2,1,0:T(1,128)} %bitcast.11, s32[1,1,64]{2,1,0:T(1,128)} %spec_h.1, s32[1,1,64]{2,1,0:T(1,128)} %occ_h.1, f32[10]{0:T(128)} %esh_h.1, f32[10]{0:T(128)} %esc_h.1, ...), custom_call_target="tpu_custom_call" | custom-call | flops 1100000000 | bytes 400000 | tf_op jit(solution)/shard_map/pallas_call | solution.py:369
  29.7 0.7 %shard_map.113 = (f32[1,1,64]{2,1,0:T(1,128)}, f32[1,3,1,64]{3,2,1,0:T(1,128)}, f32[1,1,64,128]{3,2,1,0:T(8,128)}) custom-call(f32[1,1,64]{2,1,0:T(1,128)S(1)} %get-tuple-element.9.a, f32[1,3,1,64]{3,2,1,0:T(1,128)S(1)} %get-tuple-element.10.b, f32[1,1,64,128]{3,2,1,0:T(8,128)S(1)} %get-tuple-element.11.c), custom_call_target="tpu_custom_call" | custom-call | tf_op jit(solution)/shard_map/pallas_call | solution.py:407

commit v4 on v3

--- a/solution.py
+++ b/solution.py
@@ -83,7 +83,7 @@
     nf_h, pos_h, spec_h, occ_h, esh_h, esc_h, rw_h, mix_h, ro_h,
     energy_o, force_o, fgrad_o,
     nf, pos, spec, occ, esh, esc, rw, mix, ro,
-    feat, posb, rows, cols, basis, geo, dbs, coeff, coeff_t, near, pieces, gsend, precv, grecv, giacc,
+    feat, posb, rows, cols, basis, geo, dbs, coeff, coeff_t, mix_t, feat_t, near, pieces, gsend, precv, grecv, giacc,
     ps_sem, pr_sem, fs_sem, fr_sem, ds_sem, dr_sem, gs_sem, gr_sem, in_sem,
 ):
     nx, ny = lax.axis_size("gx"), lax.axis_size("gy")
@@ -216,6 +216,8 @@
             rows[a : a + 1, pl.ds(tile * C, C)] = pair
         pair_tile(tile, False)
 
+    mix_t[...] = mix[...].T
+
     neighbour_tile(3)
     neighbour_tile(2)
     for s in (7, 6, 5, 4):
@@ -223,6 +225,8 @@
     near[...] = jnp.dot(
         basis[:, pl.ds(2 * C, 3 * C)], feat[4:10].reshape(6 * S, C), preferred_element_type=F32
     )
+    for tile in (2, 3, 4):
+        feat_t[:, pl.ds(tile * C, C)] = feat[2 * tile : 2 * tile + 2].reshape(C, C).T
     neighbour_tile(1)
     neighbour_tile(0)
     for s in (3, 2, 1, 0):
@@ -230,6 +234,8 @@
     sums = near[...] + jnp.dot(
         basis[:, pl.ds(0, 2 * C)], feat[0:4].reshape(4 * S, C), preferred_element_type=F32
     )
+    for tile in (0, 1):
+        feat_t[:, pl.ds(tile * C, C)] = feat[2 * tile : 2 * tile + 2].reshape(C, C).T
     weight = [[rw[d, n : n + 1, :] for d in range(3)] for n in range(NB)]
     amp = []
     for lm in range(9):
@@ -246,7 +252,7 @@
     sigma = jax.nn.sigmoid(pre)
     readout = ro[...]
     dpre = (coef_col * readout * sigma * (1.0 + pre * (1.0 - sigma))).astype(BF16)
-    dinv = lax.dot_general(dpre, mix[...], (((1,), (1,)), ((), ())), preferred_element_type=F32)
+    dinv = jnp.dot(dpre, mix_t[...], preferred_element_type=F32)
     for lm in range(9):
         d = DEGREE[lm]
         damp = dinv[:, d * C : (d + 1) * C]
@@ -306,9 +312,7 @@
         return jnp.dot(coeff_t[...], basis[:, lanes], preferred_element_type=F32)
 
     for half in range(2):
-        dbs[...] = lax.dot_general(
-            coeff[...], feat[half * 4 : half * 4 + 4].reshape(4 * S, C), (((1,), (1,)), ((), ())), preferred_element_type=F32
-        )
+        dbs[...] = jnp.dot(coeff[...], feat_t[:, pl.ds(half * 2 * C, 2 * C)], preferred_element_type=F32)
         part = feature_part(pl.ds(half * 2 * C, 2 * C)).astype(BF16).T
         for i in range(4):
             s = half * 4 + i
@@ -321,9 +325,7 @@
                 grad_copy(s, target[s]).start()
 
     own_part = feature_part(pl.ds(4 * C, C)).T
-    dbs[:, pl.ds(0, C)] = lax.dot_general(
-        coeff[...], feat[8:10].reshape(2 * S, C), (((1,), (1,)), ((), ())), preferred_element_type=F32
-    )
+    dbs[:, pl.ds(0, C)] = jnp.dot(coeff[...], feat_t[:, pl.ds(4 * C, C)], preferred_element_type=F32)
     own_grad = force_tile(4, 0)
     centre_rows = [jnp.sum(giacc[a].T, axis=0, keepdims=True) for a in range(3)]
     energy_row = jnp.sum((pre * sigma * readout).T, axis=0, keepdims=True)
@@ -390,6 +392,8 @@
             pltpu.VMEM((K * S, 2 * C), F32),
             pltpu.VMEM((K * S, C), BF16),
             pltpu.VMEM((C, K * S), BF16),
+            pltpu.VMEM((C, 3 * C), BF16),
+            pltpu.VMEM((C, LANES), BF16),
             pltpu.VMEM((K * S, C), F32),
             pltpu.VMEM((8, S, C), BF16),
             pltpu.VMEM((4, 8, C), F32),

time: 30.5 us -> 30.5 us (level)
  no operation moved by 1% of the time
where the time goes in v4:
time: 30.5 us; the launch traced here: 30.3 us
  Pallas kernels  29.7 us (97%)
  between operations  0.64 us (2%)
    pallas_call x1, Pallas kernels, shards(): pl.pallas_call(kernel, out_shape=shapes, in_specs=[hbm] * 9, out_specs=(v...  29.1 us
    pallas_call x1, Pallas kernels, shards(): pl.pallas_call(emit, out_shape=shapes, in_specs=[vmem] * 3, out_specs=(hb...  0.65 us

profile of v4, /device:TPU:1, one launch (start us, length us, event | category | flops | bytes accessed | tf_op | source)
XLA Modules:
  0.0 30.3 jit_solution(10370456244788287844)
XLA Ops:
  0.6 29.1 %shard_map.112 = (f32[1,1,64]{2,1,0:T(1,128)S(1)}, f32[1,3,1,64]{3,2,1,0:T(1,128)S(1)}, f32[1,1,64,128]{3,2,1,0:T(8,128)S(1)}) custom-call(bf16[1,1,64,128]{3,2,1,0:T(8,128)(2,1)} %bitcast.9, f32[1,3,1,64]{3,2,1,0:T(1,128)} %bitcast.11, s32[1,1,64]{2,1,0:T(1,128)} %spec_h.1, s32[1,1,64]{2,1,0:T(1,128)} %occ_h.1, f32[10]{0:T(128)} %esh_h.1, f32[10]{0:T(128)} %esc_h.1, ...), custom_call_target="tpu_custom_call" | custom-call | flops 1100000000 | bytes 400000 | tf_op jit(solution)/shard_map/pallas_call | solution.py:371
  29.7 0.7 %shard_map.113 = (f32[1,1,64]{2,1,0:T(1,128)}, f32[1,3,1,64]{3,2,1,0:T(1,128)}, f32[1,1,64,128]{3,2,1,0:T(8,128)}) custom-call(f32[1,1,64]{2,1,0:T(1,128)S(1)} %get-tuple-element.9.a, f32[1,3,1,64]{3,2,1,0:T(1,128)S(1)} %get-tuple-element.10.b, f32[1,1,64,128]{3,2,1,0:T(8,128)S(1)} %get-tuple-element.11.c), custom_call_target="tpu_custom_call" | custom-call | tf_op jit(solution)/shard_map/pallas_call | solution.py:411
